TPU v7x, 256 devices: a whole 4x4x8 slice. The times are simulated.
256 devices in a mesh: row: 16 (over x_hi, z), col: 16 (over x_lo, y, core).
Axes of the slice: x: 4 (x_hi: 2, x_lo: 2; x = x_hi * 2 + x_lo), y: 4, z: 8, core: 2. Of those that a mesh axis runs over, the one named last changes fastest.
Arguments:
- target_state: float32 [12, 32768], P(None, ('row', 'col')), may hold values from -6 to 6
- target_mass: float32 [32768], P(('row', 'col')), may hold values from 0.25 to 4
- source_state: float32 [12, 32768], P(None, ('row', 'col')), may hold values from -6 to 6
- source_mass: float32 [32768], P(('row', 'col')), may hold values from 0.25 to 4
Outputs:
- target_next: float32 [12, 32768], P(None, ('row', 'col'))
- source_pull: float32 [6, 32768], P(None, ('row', 'col'))
All inputs are finite; a program needn't handle non-finite values.
Results may differ from a plain program's by a relative error of at most 0.0003.
Values sent between devices are 32-bit elements; how exact they have to be, the bound alone decides.
A program may use at most 64 MiB of HBM per device.

v0:
```python
import jax
import jax.numpy as jnp
from jax import lax
from jax.sharding import PartitionSpec as P

STEP = 0.25
SOFTEN = 0.0025


def predict(state):
    position = state[0:3]
    velocity = state[3:6]
    accel = state[6:9]
    jerks = state[9:12]
    new_position = position + STEP * (velocity + STEP * (0.5 * accel + STEP / 6.0 * jerks))
    new_velocity = velocity + STEP * (accel + 0.5 * STEP * jerks)
    return jnp.concatenate([new_position, new_velocity], axis=0)


def interact(targets, target_weight, sources, source_weight):
    offset = sources[0:3, None, :] - targets[0:3, :, None]
    relative = sources[3:6, None, :] - targets[3:6, :, None]
    square = jnp.sum(offset * offset, axis=0) + SOFTEN
    inverse = lax.rsqrt(square)
    inverse_two = inverse * inverse
    inverse_three = inverse * inverse_two
    radial = 3.0 * jnp.sum(offset * relative, axis=0) * inverse_two
    change = relative - radial[None] * offset
    on_target = inverse_three * source_weight[None, :]
    on_source = inverse_three * target_weight[:, None]
    target_terms = jnp.concatenate(
        [jnp.sum(offset * on_target[None], axis=2), jnp.sum(change * on_target[None], axis=2)],
        axis=0,
    )
    source_terms = -jnp.concatenate(
        [jnp.sum(offset * on_source[None], axis=1), jnp.sum(change * on_source[None], axis=1)],
        axis=0,
    )
    return (target_terms, source_terms)


def correct(state, totals):
    position = state[0:3]
    velocity = state[3:6]
    accel = state[6:9]
    jerks = state[9:12]
    new_accel = totals[0:3]
    new_jerks = totals[3:6]
    new_velocity = (
        velocity + 0.5 * STEP * (accel + new_accel) + STEP * STEP / 12.0 * (jerks - new_jerks)
    )
    new_position = (
        position + 0.5 * STEP * (velocity + new_velocity) + STEP * STEP / 12.0 * (accel - new_accel)
    )
    return jnp.concatenate([new_position, new_velocity, new_accel, new_jerks], axis=0)


def shards(target_state, target_mass, source_state, source_mass):
    devices_all = lax.axis_size("row") * lax.axis_size("col")
    total_targets = target_mass.shape[0] * devices_all
    total_sources = source_mass.shape[0] * devices_all
    gathered_state, gathered_mass = (
        lax.all_gather(target_state, "col", axis=1, tiled=True),
        lax.all_gather(target_mass, "col", axis=0, tiled=True),
    )
    targets = predict(gathered_state)
    source_gathered, source_masses = (
        lax.all_gather(source_state, "row", axis=1, tiled=True),
        lax.all_gather(source_mass, "row", axis=0, tiled=True),
    )
    sources = predict(source_gathered)
    target_weight = gathered_mass / total_targets
    source_weight = source_masses / total_sources
    column_length = sources.shape[1]
    width = min(256, column_length)
    count = column_length // width
    blocks = sources.reshape(6, count, width).transpose(1, 0, 2)
    weights = source_weight.reshape(count, width)

    def advance(total, item):
        block, weight = item
        target_terms, source_terms = interact(targets, target_weight, block, weight)
        return (total + target_terms, source_terms)

    partial_totals, pulls = lax.scan(
        advance, jnp.zeros((6, targets.shape[1]), jnp.float32), (blocks, weights)
    )
    pull_partial = pulls.transpose(1, 0, 2).reshape(6, column_length)
    totals = lax.psum_scatter(partial_totals, "col", scatter_dimension=1, tiled=True)
    source_pull = lax.psum_scatter(pull_partial, "row", scatter_dimension=1, tiled=True)
    return (correct(target_state, totals), source_pull)


def solution(mesh):
    placed = (
        P(None, ("row", "col")),
        P(("row", "col")),
        P(None, ("row", "col")),
        P(("row", "col")),
    )
    return jax.shard_map(
        shards,
        mesh=mesh,
        in_specs=placed,
        out_specs=(P(None, ("row", "col")), P(None, ("row", "col"))),
        check_vma=False,
    )
```

profile of v0, /device:TPU:1, one launch (start us, length us, event | category | flops | bytes accessed | tf_op | source)
XLA Modules:
  0.0 397.7 jit_solution(8836641661894508177)
XLA Ops:
  7.2 38.7 %all_gather.12 = f32[12,2048]{1,0:T(8,128)S(1)} all-gather(f32[12,128]{1,0:T(8,128)} %param.8), channel_id=1, replica_groups=mesh['row'=16,'col'=16] {'row'}, dimensions={1}, use_global_device_ids=true | all-gather | bytes 104448 | tf_op jit(solution)/shard_map/all_gather | solution.py:68
  46.0 27.0 %all_gather.13 = f32[12,2048]{1,0:T(8,128)S(1)} all-gather(f32[12,128]{1,0:T(8,128)} %param.6), channel_id=1, replica_groups=mesh['row'=16,'col'=16] {'col'}, dimensions={1}, use_global_device_ids=true | all-gather | bytes 104448 | tf_op jit(solution)/shard_map/all_gather | solution.py:63
  73.0 28.6 %all-gather = f32[16,1,128]{2,1,0:T(1,128)S(1)} all-gather(f32[1,1,128]{2,1,0:T(1,128)} %bitcast.30), channel_id=1, replica_groups=mesh['row'=16,'col'=16] {'row'}, dimensions={0}, use_global_device_ids=true | all-gather | bytes 8704 | tf_op jit(solution)/shard_map/all_gather | solution.py:69
  101.6 23.3 %all-gather.1 = f32[16,1,128]{2,1,0:T(1,128)S(1)} all-gather(f32[1,1,128]{2,1,0:T(1,128)} %bitcast.31), channel_id=1, replica_groups=mesh['row'=16,'col'=16] {'col'}, dimensions={0}, use_global_device_ids=true | all-gather | bytes 8704 | tf_op jit(solution)/shard_map/all_gather | solution.py:64
  124.9 58.1 %while.13 = (s32[]{:T(128)}, f32[6,2048]{1,0:T(8,128)S(1)}, f32[8,6,256]{2,1,0:T(8,128)S(1)}, f32[8,6,256]{2,1,0:T(8,128)S(1)}, f32[3,2048]{1,0:T(4,128)S(1)}, /...) while((s32[]{:T(128)}, f32[6,2048]{1,0:T(8,128)S(1)}, ...), condition=%wide.region_7.8_spmd.clone, body=%wide.region_0.7_spmd.clone.sunk | while | flops 30959108 | bytes 21324944 | solution.py:85
  125.0 2.2 fusion.15
  127.2 0.6 fusion.16
  127.8 4.3 %fusion.17 = (f32[3,256]{1,0:T(4,128)S(1)}, f32[3,2048]{1,0:T(4,128)S(1)}, f32[3,2048]{1,0:T(4,128)S(1)}, f32[3,256]{1,0:T(4,128)S(1)}) fusion(f32[2048,256]{1,0:T(8,128)S(1)} %get-tuple-element.171, f32[2048,256]{1,0:T(8,128)S(1)} %get-tuple-element.172, f32[3,2048]{1,0:T(4,128)S(1)} %get-tuple-element.206, f32[3,256]{1,0:T(4,128)S(1)} %get-tuple-element.168, ...), kind=kLoop, calls=%fused_computation.12.clone.1 | loop fusion | flops 18860544 | bytes 6402048 | tf_op jit(solution)/shard_map/while/body/eval_jaxpr/reduce_sum | solution.py:36
  132.2 2.2 fusion.15
  134.5 0.6 fusion.16
  135.1 4.3 %fusion.17 = (f32[3,256]{1,0:T(4,128)S(1)}, f32[3,2048]{1,0:T(4,128)S(1)}, f32[3,2048]{1,0:T(4,128)S(1)}, f32[3,256]{1,0:T(4,128)S(1)}) fusion(f32[2048,256]{1,0:T(8,128)S(1)} %get-tuple-element.171, f32[2048,256]{1,0:T(8,128)S(1)} %get-tuple-element.172, f32[3,2048]{1,0:T(4,128)S(1)} %get-tuple-element.206, f32[3,256]{1,0:T(4,128)S(1)} %get-tuple-element.168, ...), kind=kLoop, calls=%fused_computation.12.clone.1 | loop fusion | flops 18860544 | bytes 6402048 | tf_op jit(solution)/shard_map/while/body/eval_jaxpr/reduce_sum | solution.py:36
  139.5 2.2 fusion.15
  141.7 0.6 fusion.16
  142.3 4.3 %fusion.17 = (f32[3,256]{1,0:T(4,128)S(1)}, f32[3,2048]{1,0:T(4,128)S(1)}, f32[3,2048]{1,0:T(4,128)S(1)}, f32[3,256]{1,0:T(4,128)S(1)}) fusion(f32[2048,256]{1,0:T(8,128)S(1)} %get-tuple-element.171, f32[2048,256]{1,0:T(8,128)S(1)} %get-tuple-element.172, f32[3,2048]{1,0:T(4,128)S(1)} %get-tuple-element.206, f32[3,256]{1,0:T(4,128)S(1)} %get-tuple-element.168, ...), kind=kLoop, calls=%fused_computation.12.clone.1 | loop fusion | flops 18860544 | bytes 6402048 | tf_op jit(solution)/shard_map/while/body/eval_jaxpr/reduce_sum | solution.py:36
  146.8 2.2 fusion.15
  149.0 0.6 fusion.16
  149.6 4.3 %fusion.17 = (f32[3,256]{1,0:T(4,128)S(1)}, f32[3,2048]{1,0:T(4,128)S(1)}, f32[3,2048]{1,0:T(4,128)S(1)}, f32[3,256]{1,0:T(4,128)S(1)}) fusion(f32[2048,256]{1,0:T(8,128)S(1)} %get-tuple-element.171, f32[2048,256]{1,0:T(8,128)S(1)} %get-tuple-element.172, f32[3,2048]{1,0:T(4,128)S(1)} %get-tuple-element.206, f32[3,256]{1,0:T(4,128)S(1)} %get-tuple-element.168, ...), kind=kLoop, calls=%fused_computation.12.clone.1 | loop fusion | flops 18860544 | bytes 6402048 | tf_op jit(solution)/shard_map/while/body/eval_jaxpr/reduce_sum | solution.py:36
  154.0 2.2 fusion.15
  156.3 0.6 fusion.16
  156.9 4.3 %fusion.17 = (f32[3,256]{1,0:T(4,128)S(1)}, f32[3,2048]{1,0:T(4,128)S(1)}, f32[3,2048]{1,0:T(4,128)S(1)}, f32[3,256]{1,0:T(4,128)S(1)}) fusion(f32[2048,256]{1,0:T(8,128)S(1)} %get-tuple-element.171, f32[2048,256]{1,0:T(8,128)S(1)} %get-tuple-element.172, f32[3,2048]{1,0:T(4,128)S(1)} %get-tuple-element.206, f32[3,256]{1,0:T(4,128)S(1)} %get-tuple-element.168, ...), kind=kLoop, calls=%fused_computation.12.clone.1 | loop fusion | flops 18860544 | bytes 6402048 | tf_op jit(solution)/shard_map/while/body/eval_jaxpr/reduce_sum | solution.py:36
  161.3 2.2 fusion.15
  163.5 0.6 fusion.16
  164.1 4.3 %fusion.17 = (f32[3,256]{1,0:T(4,128)S(1)}, f32[3,2048]{1,0:T(4,128)S(1)}, f32[3,2048]{1,0:T(4,128)S(1)}, f32[3,256]{1,0:T(4,128)S(1)}) fusion(f32[2048,256]{1,0:T(8,128)S(1)} %get-tuple-element.171, f32[2048,256]{1,0:T(8,128)S(1)} %get-tuple-element.172, f32[3,2048]{1,0:T(4,128)S(1)} %get-tuple-element.206, f32[3,256]{1,0:T(4,128)S(1)} %get-tuple-element.168, ...), kind=kLoop, calls=%fused_computation.12.clone.1 | loop fusion | flops 18860544 | bytes 6402048 | tf_op jit(solution)/shard_map/while/body/eval_jaxpr/reduce_sum | solution.py:36
  168.5 2.2 fusion.15
  171.4 4.3 %fusion.17 = (f32[3,256]{1,0:T(4,128)S(1)}, f32[3,2048]{1,0:T(4,128)S(1)}, f32[3,2048]{1,0:T(4,128)S(1)}, f32[3,256]{1,0:T(4,128)S(1)}) fusion(f32[2048,256]{1,0:T(8,128)S(1)} %get-tuple-element.171, f32[2048,256]{1,0:T(8,128)S(1)} %get-tuple-element.172, f32[3,2048]{1,0:T(4,128)S(1)} %get-tuple-element.206, f32[3,256]{1,0:T(4,128)S(1)} %get-tuple-element.168, ...), kind=kLoop, calls=%fused_computation.12.clone.1 | loop fusion | flops 18860544 | bytes 6402048 | tf_op jit(solution)/shard_map/while/body/eval_jaxpr/reduce_sum | solution.py:36
  175.8 2.2 fusion.15
  178.7 4.3 %fusion.17 = (f32[3,256]{1,0:T(4,128)S(1)}, f32[3,2048]{1,0:T(4,128)S(1)}, f32[3,2048]{1,0:T(4,128)S(1)}, f32[3,256]{1,0:T(4,128)S(1)}) fusion(f32[2048,256]{1,0:T(8,128)S(1)} %get-tuple-element.171, f32[2048,256]{1,0:T(8,128)S(1)} %get-tuple-element.172, f32[3,2048]{1,0:T(4,128)S(1)} %get-tuple-element.206, f32[3,256]{1,0:T(4,128)S(1)} %get-tuple-element.168, ...), kind=kLoop, calls=%fused_computation.12.clone.1 | loop fusion | flops 18860544 | bytes 6402048 | tf_op jit(solution)/shard_map/while/body/eval_jaxpr/reduce_sum | solution.py:36
  183.8 0.7 reduce-scatter.5.cloned.1.call-update
  184.4 53.3 %reduce-scatter.3.cloned.1.call-done = f32[6,128]{1,0:T(8,128)} async-done(((f32[6,2048]{1,0:T(8,128)}), f32[6,128]{1,0:T(8,128)}) %reduce-scatter.3.cloned.1.call-update) | async-done | bytes 3088 | tf_op jit(solution)/shard_map/reduce_scatter | solution.py:89
  237.8 0.8 multiply_add_fusion.2
  238.5 1.3 pad_maximum_fusion.1
  239.8 151.1 %reduce-scatter.5.cloned.1.call-done = f32[6,128]{1,0:T(8,128)} async-done(((f32[6,2048]{1,0:T(8,128)}), f32[6,128]{1,0:T(8,128)}) %reduce-scatter.5.cloned.1.call-update) | async-done | bytes 3088 | tf_op jit(solution)/shard_map/reduce_scatter | solution.py:90
  (51 shorter events, 2.5 us)
Async XLA Ops:
  7.2 230.6 %reduce-scatter.3.cloned.1.call-start = ((), (), s32[]{:S(2)}) async-start(), calls=%async_computation.2 | async-start | bytes 69632 | tf_op jit(solution)/shard_map/reduce_scatter | solution.py:89
  124.9 112.8 %copy-start.2 = (f32[12,128]{1,0:T(8,128)S(1)}, f32[12,128]{1,0:T(8,128)}, u32[]{:S(2)}) copy-start(f32[12,128]{1,0:T(8,128)} %param.6) | copy-start | bytes 18436
  183.0 0.6 copy-start
  183.1 0.7 copy-start.1
  183.7 207.2 %reduce-scatter.5.cloned.1.call-start = ((), (), s32[]{:S(2)}) async-start(), calls=%async_computation.3 | async-start | bytes 69632 | tf_op jit(solution)/shard_map/reduce_scatter | solution.py:90
Sparse Core Ops, SparseCore 0:
  183.8 53.8 reduce-scatter.2
  242.4 148.4 reduce-scatter.4
where the time goes:
time: 402 us; the launch traced here: 398 us
  waiting for transfers between devices  205 us (51%)
  blocking collectives  118 us (29%)
  other arithmetic  59.6 us (15%)
  between operations  14.1 us (4%)
    reduce_scatter x1, waiting for transfers between devices, shards(): lax.psum_scatter(pull_partial, 'row', scatter_dimension=1, tiled=True)  151 us
    reduce_scatter x1, waiting for transfers between devices, shards(): lax.psum_scatter(partial_totals, 'col', scatter_dimension=1, tiled=True)  53.3 us
    all_gather x1, blocking collectives, shards(): lax.all_gather(source_state, 'row', axis=1, tiled=True)  38.7 us
    reduce_sum x8, other arithmetic, interact(): jnp.sum(change * on_source[None], axis=1)  34.5 us
    all_gather x1, blocking collectives, shards(): lax.all_gather(source_mass, 'row', axis=0, tiled=True)  28.6 us
    all_gather x1, blocking collectives, shards(): lax.all_gather(target_state, 'col', axis=1, tiled=True)  27 us
    all_gather x1, blocking collectives, shards(): lax.all_gather(target_mass, 'col', axis=0, tiled=True)  23.3 us
    reduce_sum x8, other arithmetic, interact(): square = jnp.sum(offset * offset, axis=0) + SOFTEN  17.7 us
  transfers between devices with their start and end apart: 2, of which 2 were waited for; matrix products, arithmetic and copies ran while one was open for 1% of the time, Pallas kernels for 0%

commit v1 on v0

v1 whole, which is shorter than its diff:
```python
import functools

import jax
import jax.numpy as jnp
from jax import lax
from jax.experimental import pallas as pl
from jax.experimental.pallas import tpu as pltpu
from jax.sharding import PartitionSpec as P

STEP = 0.25
SOFTEN = 0.0025
MESH = pl.DeviceIdType.MESH
f32, bf16 = jnp.float32, jnp.bfloat16
OWN = 128


def dot(a, b, ca, cb):
    return lax.dot_general(a, b, (((ca,), (cb,)), ((), ())), preferred_element_type=f32)


def pieces(x):
    high = x.astype(bf16).astype(f32)
    rest = x - high
    mid = rest.astype(bf16).astype(f32)
    return high, mid, (rest - mid).astype(bf16).astype(f32)


def halves(x):
    high = x.astype(bf16)
    return high, (x - high.astype(f32)).astype(bf16)


def predict(state, mass):
    x, v, a, j = state[0:3], state[3:6], state[6:9], state[9:12]
    xp = x + STEP * (v + STEP * (0.5 * a + STEP / 6.0 * j))
    vp = v + STEP * (a + 0.5 * STEP * j)
    return jnp.concatenate([xp, vp, jnp.ones_like(mass), mass], axis=0)


def moments(tile):
    row = lax.broadcasted_iota(jnp.int32, tile.shape, 0)
    mass = jnp.broadcast_to(tile[7:8], tile.shape)
    first = jnp.where(row < 7, tile * mass, 0.0)
    moved = pltpu.roll(first, 3, 0)
    second = jnp.where(row == 7, mass, jnp.where((row >= 3) & (row < 6), -moved, 0.0))
    zero = jnp.zeros_like(tile)
    return (
        jnp.concatenate([*pieces(first), zero], axis=0).astype(bf16),
        jnp.concatenate([*pieces(second), zero], axis=0).astype(bf16),
    )


def resolve(total, tile):
    x, v = tile[0:3], tile[3:6]
    accel = total[0:3] - x * total[6:7]
    jerk = total[3:6] - v * total[6:7] + x * total[7:8]
    return accel, jerk


def kernel(rows, cols, ts_ref, tm_ref, ss_ref, sm_ref, next_ref, pull_ref,
           tgat, sgat, ft, fs, rc, rg, tc, tg, xb, xs, osum, tsum, pt, ps, qt, qs, send, recv):
    row, col = lax.axis_index("row"), lax.axis_index("col")
    BI, BK = 256, 512
    nt, ns = cols * OWN, rows * OWN

    def in_col(e):
        return (row, lax.rem(col + e, cols))

    def in_row(e):
        return (lax.rem(row + e, rows), col)

    barrier = pltpu.get_barrier_semaphore()
    for e in range(1, cols):
        pl.semaphore_signal(barrier, inc=1, device_id=in_col(e), device_id_type=MESH)
    for e in range(1, rows):
        pl.semaphore_signal(barrier, inc=1, device_id=in_row(e), device_id_type=MESH)

    tgat[cols - 1] = predict(ts_ref[...], tm_ref[...] * (1.0 / (nt * rows)))
    sgat[rows - 1] = predict(ss_ref[...], sm_ref[...] * (1.0 / (ns * cols)))
    osum[...] = jnp.zeros_like(osum)
    tsum[...] = jnp.zeros_like(tsum)
    pl.semaphore_wait(barrier, cols + rows - 2)

    def t_gather(e):
        return pltpu.make_async_remote_copy(
            src_ref=tgat.at[cols - 1], dst_ref=tgat.at[cols - 1 - e], send_sem=send.at[0, e],
            recv_sem=recv.at[0, cols - 1 - e], device_id=in_col(e), device_id_type=MESH)

    def s_gather(e):
        return pltpu.make_async_remote_copy(
            src_ref=sgat.at[rows - 1], dst_ref=sgat.at[rows - 1 - e], send_sem=send.at[1, e],
            recv_sem=recv.at[1, rows - 1 - e], device_id=in_row(e), device_id_type=MESH)

    def t_return(d):
        return pltpu.make_async_remote_copy(
            src_ref=pt.at[d], dst_ref=qt.at[cols - 2 - d], send_sem=send.at[2, d],
            recv_sem=recv.at[2, cols - 2 - d], device_id=in_col(d + 1), device_id_type=MESH)

    def s_return(d):
        return pltpu.make_async_remote_copy(
            src_ref=ps.at[d], dst_ref=qs.at[rows - 2 - d], send_sem=send.at[3, d],
            recv_sem=recv.at[3, rows - 2 - d], device_id=in_row(d + 1), device_id_type=MESH)

    for e in range(1, rows):
        s_gather(e).start()
    for e in range(1, cols):
        t_gather(e).start()

    zeros = jnp.zeros((OWN - 48, OWN), f32)

    def prepare_source(d):
        tile = sgat[d]
        at = pl.ds(pl.multiple_of(d * OWN, OWN), OWN)
        rc[:, at], rg[:, at] = moments(tile)
        x, v = tile[0:3], tile[3:6]
        vec = jnp.concatenate([-3.0 * v, -3.0 * x, 3.0 * jnp.sum(x * v, axis=0, keepdims=True), tile[6:7]], axis=0)
        h, m, l = pieces(vec)
        fs[:, at] = jnp.concatenate([h, m, h, m, l, h, zeros], axis=0).astype(bf16)
        xs[:, at] = tile

    def prepare_target(d):
        tile = tgat[d]
        at = pl.ds(pl.multiple_of(d * OWN, OWN), OWN)
        tc[:, at], tg[:, at] = moments(tile)
        x, v = tile[0:3], tile[3:6]
        vec = jnp.concatenate([x, v, tile[6:7], 3.0 * jnp.sum(x * v, axis=0, keepdims=True)], axis=0)
        h, m, l = pieces(vec)
        ft[at, :] = jnp.concatenate([h, h, m, m, h, l, zeros], axis=0).T.astype(bf16)
        for c in range(3):
            xb[at, c * OWN:(c + 1) * OWN] = jnp.broadcast_to(tile[c:c + 1], (OWN, OWN)).T

    def arrive_source(d, _):
        @pl.when(d < rows - 1)
        def _():
            s_gather(rows - 1 - d).wait_recv()
        prepare_source(d)
        return 0

    def arrive_target(d, _):
        @pl.when(d < cols - 1)
        def _():
            t_gather(cols - 1 - d).wait_recv()
        prepare_target(d)
        return 0

    lax.fori_loop(0, rows, arrive_source, 0)
    lax.fori_loop(0, cols, arrive_target, 0)

    def tile(i0, k0):
        i, k = pl.ds(i0, BI), pl.ds(k0, BK)
        dw = dot(ft[i, :], fs[:, k], 1, 0)
        s = SOFTEN
        for c in range(3):
            left = xb[i, c * OWN:(c + 1) * OWN]
            d = xs[c:c + 1, k] - jnp.concatenate([left] * (BK // OWN), axis=1)
            s = d * d + s
        q = lax.rsqrt(s)
        q2 = q * q
        c = q * q2
        g = (dw * q2) * c
        ch, cl = halves(c)
        gh, gl = halves(g)
        tci, tgi, rck, rgk = tc[:, i], tg[:, i], rc[:, k], rg[:, k]
        osum[:, k] += dot(jnp.concatenate([tci, tci, tgi, tgi], axis=1),
                          jnp.concatenate([ch, cl, gh, gl], axis=0), 1, 0)
        tsum[:, i] += dot(jnp.concatenate([rck, rck, rgk, rgk], axis=1),
                          jnp.concatenate([ch, cl, gh, gl], axis=1), 1, 1)

    def fold(total):
        return total[0:8] + total[8:16] + total[16:24]

    def strip(n, _):
        i0 = pl.multiple_of(n * BI, BI)

        def part(p, _):
            for u in range(2):
                tile(i0, pl.multiple_of((p * 2 + u) * BK, BK))
            return 0

        lax.fori_loop(0, ns // (2 * BK), part, 0)
        for u in range(BI // OWN):
            d = n * (BI // OWN) + u
            pt[d] = fold(tsum[:, pl.ds(pl.multiple_of(d * OWN, OWN), OWN)])

            @pl.when(d < cols - 1)
            def _():
                t_return(d).start()
        return 0

    lax.fori_loop(0, nt // BI, strip, 0)
    for d in range(rows):
        ps[d] = fold(osum[:, d * OWN:(d + 1) * OWN])
        if d < rows - 1:
            s_return(d).start()

    def settle_target(d, total):
        t_return(cols - 2 - d).wait_recv()
        return total + qt[d]

    total = lax.fori_loop(0, cols - 1, settle_target, pt[cols - 1])
    a1, j1 = resolve(total, tgat[cols - 1])
    x, v, a, j = ts_ref[0:3], ts_ref[3:6], ts_ref[6:9], ts_ref[9:12]
    v1 = v + 0.5 * STEP * (a + a1) + STEP * STEP / 12.0 * (j - j1)
    x1 = x + 0.5 * STEP * (v + v1) + STEP * STEP / 12.0 * (a - a1)
    next_ref[...] = jnp.concatenate([x1, v1, a1, j1], axis=0)

    def settle_source(d, total):
        s_return(rows - 2 - d).wait_recv()
        return total + qs[d]

    total = lax.fori_loop(0, rows - 1, settle_source, ps[rows - 1])
    pull_ref[...] = jnp.concatenate(resolve(total, sgat[rows - 1]), axis=0)

    for e in range(1, rows):
        s_gather(e).wait_send()
        s_return(e - 1).wait_send()
    for e in range(1, cols):
        t_gather(e).wait_send()
        t_return(e - 1).wait_send()


def solution(mesh):
    rows, cols = mesh.shape["row"], mesh.shape["col"]
    nt, ns = cols * OWN, rows * OWN
    vmem = pl.BlockSpec(memory_space=pltpu.VMEM)
    call = pl.pallas_call(
        functools.partial(kernel, rows, cols),
        out_shape=(jax.ShapeDtypeStruct((12, OWN), f32), jax.ShapeDtypeStruct((6, OWN), f32)),
        in_specs=[vmem] * 4,
        out_specs=(vmem, vmem),
        scratch_shapes=[
            pltpu.VMEM((cols, 8, OWN), f32),
            pltpu.VMEM((rows, 8, OWN), f32),
            pltpu.VMEM((nt, OWN), bf16),
            pltpu.VMEM((OWN, ns), bf16),
            pltpu.VMEM((32, ns), bf16),
            pltpu.VMEM((32, ns), bf16),
            pltpu.VMEM((32, nt), bf16),
            pltpu.VMEM((32, nt), bf16),
            pltpu.VMEM((nt, 3 * OWN), f32),
            pltpu.VMEM((8, ns), f32),
            pltpu.VMEM((32, ns), f32),
            pltpu.VMEM((32, nt), f32),
            pltpu.VMEM((cols, 8, OWN), f32),
            pltpu.VMEM((rows, 8, OWN), f32),
            pltpu.VMEM((cols, 8, OWN), f32),
            pltpu.VMEM((rows, 8, OWN), f32),
            pltpu.SemaphoreType.DMA((4, 16)),
            pltpu.SemaphoreType.DMA((4, 16)),
        ],
        compiler_params=pltpu.CompilerParams(
            collective_id=0, has_side_effects=True, vmem_limit_bytes=48 << 20),
    )

    def shards(target_state, target_mass, source_state, source_mass):
        return call(target_state, target_mass.reshape(1, OWN), source_state, source_mass.reshape(1, OWN))

    spec = P(None, ("row", "col"))
    line = P(("row", "col"))
    return jax.shard_map(shards, mesh=mesh, in_specs=(spec, line, spec, line),
                         out_specs=(spec, spec), check_vma=False)
```

time: 402 us -> 52.7 us (0.13)
  the two profiles are of different devices: /device:TPU:1 before, /device:TPU:16 now
where the time goes in v1:
time: 52.7 us; the launch traced here: 52.5 us
  Pallas kernels  48.6 us (92%)
  local copies, waits for them, and re-layouts  3.24 us (6%)
  between operations  0.66 us (1%)
    pallas_call x1, Pallas kernels, shards(): call(target_state, target_mass.reshape(1, OWN), source_state, source_mass...  48.6 us
    unnamed x10, local copies, waits for them, and re-layouts  3.24 us

profile of v1, /device:TPU:16, one launch (start us, length us, event | category | flops | bytes accessed | tf_op | source)
XLA Modules:
  0.0 52.5 jit_solution(7212070528692586145)
XLA Ops:
  0.6 0.0 copy-start.2
  0.6 0.0 copy-start.3
  0.7 0.6 %copy-done.2 = f32[128]{0:T(128)S(1)} copy-done((f32[128]{0:T(128)S(1)}, f32[128]{0:T(128)}, u32[]{:S(2)}) %copy-start.2) | copy-done | bytes 536
  1.3 0.0 copy-done.3
  1.3 0.0 copy-start
  1.3 0.7 %copy-done = f32[12,128]{1,0:T(8,128)S(1)} copy-done((f32[12,128]{1,0:T(8,128)S(1)}, f32[12,128]{1,0:T(8,128)}, u32[]{:S(2)}) %copy-start) | copy-done | bytes 6168
  2.0 0.0 copy-start.1
  2.0 0.7 %copy-done.1 = f32[12,128]{1,0:T(8,128)S(1)} copy-done((f32[12,128]{1,0:T(8,128)S(1)}, f32[12,128]{1,0:T(8,128)}, u32[]{:S(2)}) %copy-start.1) | copy-done | bytes 6168
  2.7 48.6 %shard_map.59 = (f32[12,128]{1,0:T(8,128)S(1)}, f32[6,128]{1,0:T(8,128)S(1)}) custom-call(f32[12,128]{1,0:T(8,128)S(1)} %copy-done, f32[1,128]{1,0:T(1,128)S(1)} %bitcast.2, f32[12,128]{1,0:T(8,128)S(1)} %copy-done.1, f32[1,128]{1,0:T(1,128)S(1)} %bitcast.3), custom_call_target="tpu_custom_call" | custom-call | tf_op jit(solution)/shard_map/pallas_call | solution.py:256
  51.3 0.6 %copy.8 = f32[12,128]{1,0:T(8,128)} copy(f32[12,128]{1,0:T(8,128)S(1)} %get-tuple-element.4) | data formatting | bytes 12288
  51.9 0.6 %copy.9 = f32[6,128]{1,0:T(8,128)} copy(f32[6,128]{1,0:T(8,128)S(1)} %get-tuple-element.5) | data formatting | bytes 6144
Async XLA Ops:
  0.6 0.7 %copy-start.2 = (f32[128]{0:T(128)S(1)}, f32[128]{0:T(128)}, u32[]{:S(2)}) copy-start(f32[128]{0:T(128)} %param.5) | copy-start | bytes 1540
  0.6 0.7 %copy-start.3 = (f32[128]{0:T(128)S(1)}, f32[128]{0:T(128)}, u32[]{:S(2)}) copy-start(f32[128]{0:T(128)} %param.7) | copy-start | bytes 1540
  1.3 0.7 %copy-start = (f32[12,128]{1,0:T(8,128)S(1)}, f32[12,128]{1,0:T(8,128)}, u32[]{:S(2)}) copy-start(f32[12,128]{1,0:T(8,128)} %ts_ref.1) | copy-start | bytes 18436
  2.0 0.7 %copy-start.1 = (f32[12,128]{1,0:T(8,128)S(1)}, f32[12,128]{1,0:T(8,128)}, u32[]{:S(2)}) copy-start(f32[12,128]{1,0:T(8,128)} %ss_ref.1) | copy-start | bytes 18436

commit v2 on v1

v2 whole, which is shorter than its diff:
```python
import jax
import jax.numpy as jnp
import numpy as np
from jax import lax
from jax.experimental import pallas as pl
from jax.experimental.pallas import tpu as pltpu
from jax.sharding import PartitionSpec as P

STEP = 0.25
SOFTEN = 0.0025
MESH = pl.DeviceIdType.MESH
f32, bf16 = jnp.float32, jnp.bfloat16
OWN = 128


def dot(a, b, ca, cb):
    return lax.dot_general(a, b, (((ca,), (cb,)), ((), ())), preferred_element_type=f32)


def pieces(x):
    high = x.astype(bf16).astype(f32)
    rest = x - high
    mid = rest.astype(bf16).astype(f32)
    return high, mid, (rest - mid).astype(bf16).astype(f32)


def halves(x):
    high = x.astype(bf16)
    return high, (x - high.astype(f32)).astype(bf16)


def predict(state, mass):
    x, v, a, j = state[0:3], state[3:6], state[6:9], state[9:12]
    xp = x + STEP * (v + STEP * (0.5 * a + STEP / 6.0 * j))
    vp = v + STEP * (a + 0.5 * STEP * j)
    return jnp.concatenate([xp, vp, jnp.ones_like(mass), mass], axis=0)


def moments(tile):
    row = lax.broadcasted_iota(jnp.int32, tile.shape, 0)
    mass = jnp.broadcast_to(tile[7:8], tile.shape)
    first = jnp.where(row < 7, tile * mass, 0.0)
    moved = pltpu.roll(first, 3, 0)
    second = jnp.where(row == 7, mass, jnp.where((row >= 3) & (row < 6), -moved, 0.0))
    zero = jnp.zeros_like(tile)
    return (
        jnp.concatenate([*pieces(first), zero], axis=0).astype(bf16),
        jnp.concatenate([*pieces(second), zero], axis=0).astype(bf16),
    )


def resolve(total, tile):
    x, v = tile[0:3], tile[3:6]
    accel = total[0:3] - x * total[6:7]
    jerk = total[3:6] - v * total[6:7] + x * total[7:8]
    return accel, jerk


def order(offsets, distance, groups):
    left = sorted((o for o in offsets if any(o)), key=distance)
    return groups(left) + [o for o in offsets if not any(o)]


ROW_SIZES, COL_SIZES = (2, 8), (2, 4, 2)


def offsets(sizes):
    return list(np.ndindex(*sizes))


def row_hops(o):
    return 2 * o[0] + min(o[1], 8 - o[1])


def col_hops(o):
    return o[0] + min(o[1], 4 - o[1]) + 0.5 * o[2]


def spread(near):
    return near[:4] + near[4:][::-1]


ROW_SLOTS = order(offsets(ROW_SIZES), row_hops, spread)
COL_SLOTS = order(offsets(COL_SIZES), col_hops, list)


def inverse(slots, sizes):
    return [slots.index(tuple(-a % n for a, n in zip(o, sizes))) for o in slots]


ROW_BACK, COL_BACK = inverse(ROW_SLOTS, ROW_SIZES), inverse(COL_SLOTS, COL_SIZES)
LAST = 15
BI = BK = 256


def moved(index, offset, sizes):
    out, unit = 0, 1
    for o, n in reversed(list(zip(offset, sizes))):
        out = out + lax.rem(lax.div(index, unit) + o, n) * unit
        unit *= n
    return out


def kernel(ts_hbm, tm_hbm, ss_hbm, sm_hbm, next_ref, pull_ref, ts_ref, tm_ref, ss_ref, sm_ref,
           tgat, sgat, ft, fs, rc, rg, tc, tg, xb, xs, tsum, pt, ps, qt, qs, pair, turned, send, recv, load):
    row, col = lax.axis_index("row"), lax.axis_index("col")
    row_peer = [(moved(row, o, ROW_SIZES), col) for o in ROW_SLOTS]
    col_peer = [(row, moved(col, o, COL_SIZES)) for o in COL_SLOTS]
    far = sorted([(-row_hops(ROW_SLOTS[p]), 0, p) for p in range(LAST)]
                 + [(-col_hops(COL_SLOTS[p]), 1, p) for p in range(LAST)])

    barrier = pltpu.get_barrier_semaphore()
    for _, axis, p in far:
        pl.semaphore_signal(barrier, inc=1, device_id=(row_peer, col_peer)[axis][p], device_id_type=MESH)
    loads = [pltpu.make_async_copy(a, b, load.at[n]) for n, (a, b) in enumerate(
        ((ts_hbm, ts_ref), (tm_hbm, tm_ref), (ss_hbm, ss_ref), (sm_hbm, sm_ref)))]
    for copy in loads:
        copy.start()
    tsum[...] = jnp.zeros_like(tsum)
    for copy in loads:
        copy.wait()
    tgat[LAST] = predict(ts_ref[...], tm_ref[...] * (1.0 / 32768))
    sgat[LAST] = predict(ss_ref[...], sm_ref[...] * (1.0 / 32768))
    pl.semaphore_wait(barrier, 2 * LAST)

    def copy_to(src, dst, kind, p, back, peer):
        return pltpu.make_async_remote_copy(
            src_ref=src, dst_ref=dst.at[back[p]], send_sem=send.at[kind, p],
            recv_sem=recv.at[kind, back[p]], device_id=peer[p], device_id_type=MESH)

    def arrived(src, dst, kind, p, peer):
        pltpu.make_async_remote_copy(
            src_ref=src, dst_ref=dst.at[p], send_sem=send.at[kind, 0],
            recv_sem=recv.at[kind, p], device_id=peer[0], device_id_type=MESH).wait_recv()

    gathers = [(copy_to(sgat.at[LAST], sgat, 0, p, ROW_BACK, row_peer),
                copy_to(tgat.at[LAST], tgat, 1, p, COL_BACK, col_peer))[axis] for _, axis, p in far]
    for copy in gathers:
        copy.start()
    source_returns = [copy_to(ps.at[p], qs, 2, p, ROW_BACK, row_peer) for p in range(LAST)]
    target_returns = [copy_to(pt.at[p], qt, 3, p, COL_BACK, col_peer) for p in range(LAST)]

    zeros = jnp.zeros((OWN - 48, OWN), f32)

    def prepare_source(d):
        tile = sgat[d]
        at = pl.ds(pl.multiple_of(d * OWN, OWN), OWN)
        rc[:, at], rg[:, at] = moments(tile)
        x, v = tile[0:3], tile[3:6]
        vec = jnp.concatenate([-3.0 * v, -3.0 * x, 3.0 * jnp.sum(x * v, axis=0, keepdims=True), tile[6:7]], axis=0)
        h, m, l = pieces(vec)
        fs[:, at] = jnp.concatenate([h, m, h, m, l, h, zeros], axis=0).astype(bf16)
        xs[:, at] = tile

    def prepare_target(d):
        tile = tgat[d]
        at = pl.ds(pl.multiple_of(d * OWN, OWN), OWN)
        tc[:, at], tg[:, at] = moments(tile)
        x, v = tile[0:3], tile[3:6]
        vec = jnp.concatenate([x, v, tile[6:7], 3.0 * jnp.sum(x * v, axis=0, keepdims=True)], axis=0)
        h, m, l = pieces(vec)
        ft[at, :] = jnp.concatenate([h, h, m, m, h, l, zeros], axis=0).T.astype(bf16)
        for c in range(3):
            xb[at, c * OWN:(c + 1) * OWN] = jnp.broadcast_to(tile[c:c + 1], (OWN, OWN)).T

    def arrive_targets(n, _):
        for u in range(4):
            @pl.when(n * 4 + u < LAST)
            def _():
                arrived(tgat.at[LAST], tgat, 1, n * 4 + u, col_peer)
        for u in range(4):
            prepare_target(n * 4 + u)
        return 0

    lax.fori_loop(0, 4, arrive_targets, 0)

    def fold(total):
        return total[0:8] + total[8:16] + total[16:24]

    tiles = tsum.shape[1] // BI

    def strip(n, _):
        for u in range(BK // OWN):
            p = n * (BK // OWN) + u

            @pl.when(p < LAST)
            def _():
                arrived(sgat.at[LAST], sgat, 0, p, row_peer)
        for u in range(BK // OWN):
            prepare_source(n * (BK // OWN) + u)
        k = pl.ds(pl.multiple_of(n * BK, BK), BK)
        rck, rgk, fsk = rc[:, k], rg[:, k], fs[:, k]
        r4 = jnp.concatenate([rck, rck, rgk, rgk], axis=1)
        pulls = jnp.zeros((32, BK), f32)
        for t in range(tiles + 1):
            if t < tiles:
                i = slice(t * BI, (t + 1) * BI)
                dw = dot(ft[i, :], fsk, 1, 0)
                s = SOFTEN
                for c in range(3):
                    left = xb[i, c * OWN:(c + 1) * OWN]
                    d = xs[c:c + 1, k] - jnp.concatenate([left] * (BK // OWN), axis=1)
                    s = d * d + s
                q = lax.rsqrt(s)
                q2 = q * q
                c = q * q2
                g = (dw * q2) * c
                for x, part in enumerate(halves(c) + halves(g)):
                    pair[t % 2, x] = part
                for x in range(4):
                    turned[t % 2, x] = pair[t % 2, x].T
            if t > 0:
                i = slice((t - 1) * BI, t * BI)
                tci, tgi = tc[:, i], tg[:, i]
                here = [pair[(t - 1) % 2, x] for x in range(4)]
                across = [turned[(t - 1) % 2, x] for x in range(4)]
                pulls = pulls + dot(jnp.concatenate([tci, tci, tgi, tgi], axis=1),
                                    jnp.concatenate(here, axis=0), 1, 0)
                tsum[:, i] += dot(r4, jnp.concatenate(across, axis=0), 1, 0)
        pulls = fold(pulls)
        for u in range(BK // OWN):
            ps[n * (BK // OWN) + u] = pulls[:, u * OWN:(u + 1) * OWN]
        for m in range(LAST // 2 + 1):
            @pl.when(n == m)
            def _():
                for copy in source_returns[2 * m:2 * m + 2]:
                    copy.start()
        return 0

    lax.fori_loop(0, xs.shape[1] // BK, strip, 0)
    for p in sorted(range(LAST + 1), key=lambda p: -col_hops(COL_SLOTS[p])):
        pt[p] = fold(tsum[:, p * OWN:(p + 1) * OWN])
        if p < LAST:
            target_returns[p].start()
    for copy in gathers + source_returns:
        copy.wait_send()

    for p in range(LAST):
        arrived(ps.at[0], qs, 2, p, row_peer)
    pull_ref[...] = jnp.concatenate(resolve(sum((qs[p] for p in range(LAST)), ps[LAST]), sgat[LAST]), axis=0)

    for copy in target_returns:
        copy.wait_send()
    for p in range(LAST):
        arrived(pt.at[0], qt, 3, p, col_peer)
    a1, j1 = resolve(sum((qt[p] for p in range(LAST)), pt[LAST]), tgat[LAST])
    x, v, a, j = ts_ref[0:3], ts_ref[3:6], ts_ref[6:9], ts_ref[9:12]
    v1 = v + 0.5 * STEP * (a + a1) + STEP * STEP / 12.0 * (j - j1)
    x1 = x + 0.5 * STEP * (v + v1) + STEP * STEP / 12.0 * (a - a1)
    next_ref[...] = jnp.concatenate([x1, v1, a1, j1], axis=0)


def solution(mesh):
    n = (LAST + 1) * OWN
    vmem, hbm = pl.BlockSpec(memory_space=pltpu.VMEM), pl.BlockSpec(memory_space=pl.ANY)
    slots = pltpu.VMEM((LAST + 1, 8, OWN), f32)
    call = pl.pallas_call(
        kernel,
        out_shape=(jax.ShapeDtypeStruct((12, OWN), f32), jax.ShapeDtypeStruct((6, OWN), f32)),
        in_specs=[hbm] * 4,
        out_specs=(vmem, vmem),
        scratch_shapes=[
            pltpu.VMEM((12, OWN), f32),
            pltpu.VMEM((1, OWN), f32),
            pltpu.VMEM((12, OWN), f32),
            pltpu.VMEM((1, OWN), f32),
            slots,
            slots,
            pltpu.VMEM((n, OWN), bf16),
            pltpu.VMEM((OWN, n), bf16),
            *[pltpu.VMEM((32, n), bf16)] * 4,
            pltpu.VMEM((n, 3 * OWN), f32),
            pltpu.VMEM((8, n), f32),
            pltpu.VMEM((32, n), f32),
            *[slots] * 4,
            pltpu.VMEM((2, 4, BI, BK), bf16),
            pltpu.VMEM((2, 4, BK, BI), bf16),
            pltpu.SemaphoreType.DMA((4, LAST)),
            pltpu.SemaphoreType.DMA((4, LAST)),
            pltpu.SemaphoreType.DMA((4,)),
        ],
        compiler_params=pltpu.CompilerParams(
            collective_id=0, has_side_effects=True, vmem_limit_bytes=48 << 20),
    )

    def shards(target_state, target_mass, source_state, source_mass):
        return call(target_state, target_mass.reshape(1, OWN), source_state, source_mass.reshape(1, OWN))

    spec = P(None, ("row", "col"))
    line = P(("row", "col"))
    return jax.shard_map(shards, mesh=mesh, in_specs=(spec, line, spec, line),
                         out_specs=(spec, spec), check_vma=False)
```

time: 52.7 us -> 41.6 us (0.79)
  the two profiles are of different devices: /device:TPU:16 before, /device:TPU:1 now
where the time goes in v2:
time: 41.6 us; the launch traced here: 41.4 us
  Pallas kernels  37.5 us (90%)
  local copies, waits for them, and re-layouts  3.24 us (8%)
  between operations  0.66 us (2%)
    pallas_call x1, Pallas kernels, shards(): call(target_state, target_mass.reshape(1, OWN), source_state, source_mass...  37.5 us
    unnamed x10, local copies, waits for them, and re-layouts  3.24 us

profile of v2, /device:TPU:1, one launch (start us, length us, event | category | flops | bytes accessed | tf_op | source)
XLA Modules:
  0.0 41.4 jit_solution(10000921217043016502)
XLA Ops:
  0.6 0.0 copy-start.2
  0.6 0.0 copy-start.3
  0.7 0.6 %copy-done.2 = f32[128]{0:T(128)S(1)} copy-done((f32[128]{0:T(128)S(1)}, f32[128]{0:T(128)}, u32[]{:S(2)}) %copy-start.2) | copy-done | bytes 536
  1.3 0.0 copy-done.3
  1.3 0.0 copy-start
  1.3 0.7 %copy-done = f32[12,128]{1,0:T(8,128)S(1)} copy-done((f32[12,128]{1,0:T(8,128)S(1)}, f32[12,128]{1,0:T(8,128)}, u32[]{:S(2)}) %copy-start) | copy-done | bytes 6168
  2.0 0.0 copy-start.1
  2.0 0.7 %copy-done.1 = f32[12,128]{1,0:T(8,128)S(1)} copy-done((f32[12,128]{1,0:T(8,128)S(1)}, f32[12,128]{1,0:T(8,128)}, u32[]{:S(2)}) %copy-start.1) | copy-done | bytes 6168
  2.7 37.5 %shard_map.59 = (f32[12,128]{1,0:T(8,128)S(1)}, f32[6,128]{1,0:T(8,128)S(1)}) custom-call(f32[12,128]{1,0:T(8,128)S(1)} %copy-done, f32[1,128]{1,0:T(1,128)S(1)} %bitcast.2, f32[12,128]{1,0:T(8,128)S(1)} %copy-done.1, f32[1,128]{1,0:T(1,128)S(1)} %bitcast.3), custom_call_target="tpu_custom_call" | custom-call | tf_op jit(solution)/shard_map/pallas_call | solution.py:287
  40.2 0.6 %copy.8 = f32[12,128]{1,0:T(8,128)} copy(f32[12,128]{1,0:T(8,128)S(1)} %get-tuple-element.4) | data formatting | bytes 12288
  40.8 0.6 %copy.9 = f32[6,128]{1,0:T(8,128)} copy(f32[6,128]{1,0:T(8,128)S(1)} %get-tuple-element.5) | data formatting | bytes 6144
Async XLA Ops:
  0.6 0.7 %copy-start.2 = (f32[128]{0:T(128)S(1)}, f32[128]{0:T(128)}, u32[]{:S(2)}) copy-start(f32[128]{0:T(128)} %param.5) | copy-start | bytes 1540
  0.6 0.7 %copy-start.3 = (f32[128]{0:T(128)S(1)}, f32[128]{0:T(128)}, u32[]{:S(2)}) copy-start(f32[128]{0:T(128)} %param.7) | copy-start | bytes 1540
  1.3 0.7 %copy-start = (f32[12,128]{1,0:T(8,128)S(1)}, f32[12,128]{1,0:T(8,128)}, u32[]{:S(2)}) copy-start(f32[12,128]{1,0:T(8,128)} %ts_hbm.1) | copy-start | bytes 18436
  2.0 0.7 %copy-start.1 = (f32[12,128]{1,0:T(8,128)S(1)}, f32[12,128]{1,0:T(8,128)}, u32[]{:S(2)}) copy-start(f32[12,128]{1,0:T(8,128)} %ss_hbm.1) | copy-start | bytes 18436

commit v3 on v2

--- a/solution.py
+++ b/solution.py
@@ -91,6 +91,8 @@
 ROW_BACK, COL_BACK = inverse(ROW_SLOTS, ROW_SIZES), inverse(COL_SLOTS, COL_SIZES)
 LAST = 15
 BI = BK = 256
+WIDE = 2
+SLOTS = WIDE * BK // OWN
 
 
 def moved(index, offset, sizes):
@@ -109,13 +111,13 @@
     far = sorted([(-row_hops(ROW_SLOTS[p]), 0, p) for p in range(LAST)]
                  + [(-col_hops(COL_SLOTS[p]), 1, p) for p in range(LAST)])
 
-    barrier = pltpu.get_barrier_semaphore()
-    for _, axis, p in far:
-        pl.semaphore_signal(barrier, inc=1, device_id=(row_peer, col_peer)[axis][p], device_id_type=MESH)
     loads = [pltpu.make_async_copy(a, b, load.at[n]) for n, (a, b) in enumerate(
         ((ts_hbm, ts_ref), (tm_hbm, tm_ref), (ss_hbm, ss_ref), (sm_hbm, sm_ref)))]
     for copy in loads:
         copy.start()
+    barrier = pltpu.get_barrier_semaphore()
+    for _, axis, p in far:
+        pl.semaphore_signal(barrier, inc=1, device_id=(row_peer, col_peer)[axis][p], device_id_type=MESH)
     tsum[...] = jnp.zeros_like(tsum)
     for copy in loads:
         copy.wait()
@@ -179,23 +181,27 @@
 
     tiles = tsum.shape[1] // BI
 
-    def strip(n, _):
-        for u in range(BK // OWN):
-            p = n * (BK // OWN) + u
+    def features(k):
+        rck, rgk = rc[:, k], rg[:, k]
+        return jnp.concatenate([rck, rck, rgk, rgk], axis=1)
+
+    def strips(n, _):
+        for u in range(SLOTS):
+            p = n * SLOTS + u
 
             @pl.when(p < LAST)
             def _():
                 arrived(sgat.at[LAST], sgat, 0, p, row_peer)
-        for u in range(BK // OWN):
-            prepare_source(n * (BK // OWN) + u)
-        k = pl.ds(pl.multiple_of(n * BK, BK), BK)
-        rck, rgk, fsk = rc[:, k], rg[:, k], fs[:, k]
-        r4 = jnp.concatenate([rck, rck, rgk, rgk], axis=1)
-        pulls = jnp.zeros((32, BK), f32)
-        for t in range(tiles + 1):
-            if t < tiles:
-                i = slice(t * BI, (t + 1) * BI)
-                dw = dot(ft[i, :], fsk, 1, 0)
+        for u in range(SLOTS):
+            prepare_source(n * SLOTS + u)
+        spans = [pl.ds(pl.multiple_of((n * WIDE + w) * BK, BK), BK) for w in range(WIDE)]
+        pulls = [jnp.zeros((32, BK), f32)] * WIDE
+        order = [(w, t) for w in range(WIDE) for t in range(tiles)]
+        for m in range(len(order) + 1):
+            if m < len(order):
+                w, t = order[m]
+                k, i = spans[w], slice(t * BI, (t + 1) * BI)
+                dw = dot(ft[i, :], fs[:, k], 1, 0)
                 s = SOFTEN
                 for c in range(3):
                     left = xb[i, c * OWN:(c + 1) * OWN]
@@ -206,28 +212,30 @@
                 c = q * q2
                 g = (dw * q2) * c
                 for x, part in enumerate(halves(c) + halves(g)):
-                    pair[t % 2, x] = part
+                    pair[m % 2, x] = part
                 for x in range(4):
-                    turned[t % 2, x] = pair[t % 2, x].T
-            if t > 0:
-                i = slice((t - 1) * BI, t * BI)
+                    turned[m % 2, x] = pair[m % 2, x].T
+            if m > 0:
+                w, t = order[m - 1]
+                k, i = spans[w], slice(t * BI, (t + 1) * BI)
                 tci, tgi = tc[:, i], tg[:, i]
-                here = [pair[(t - 1) % 2, x] for x in range(4)]
-                across = [turned[(t - 1) % 2, x] for x in range(4)]
-                pulls = pulls + dot(jnp.concatenate([tci, tci, tgi, tgi], axis=1),
-                                    jnp.concatenate(here, axis=0), 1, 0)
-                tsum[:, i] += dot(r4, jnp.concatenate(across, axis=0), 1, 0)
-        pulls = fold(pulls)
-        for u in range(BK // OWN):
-            ps[n * (BK // OWN) + u] = pulls[:, u * OWN:(u + 1) * OWN]
-        for m in range(LAST // 2 + 1):
+                here = [pair[(m - 1) % 2, x] for x in range(4)]
+                across = [turned[(m - 1) % 2, x] for x in range(4)]
+                pulls[w] = pulls[w] + dot(jnp.concatenate([tci, tci, tgi, tgi], axis=1),
+                                          jnp.concatenate(here, axis=0), 1, 0)
+                tsum[:, i] += dot(features(k), jnp.concatenate(across, axis=0), 1, 0)
+        for w in range(WIDE):
+            folded = fold(pulls[w])
+            for u in range(BK // OWN):
+                ps[n * SLOTS + w * (BK // OWN) + u] = folded[:, u * OWN:(u + 1) * OWN]
+        for m in range(LAST // SLOTS + 1):
             @pl.when(n == m)
             def _():
-                for copy in source_returns[2 * m:2 * m + 2]:
+                for copy in source_returns[SLOTS * m:SLOTS * m + SLOTS]:
                     copy.start()
         return 0
 
-    lax.fori_loop(0, xs.shape[1] // BK, strip, 0)
+    lax.fori_loop(0, xs.shape[1] // (WIDE * BK), strips, 0)
     for p in sorted(range(LAST + 1), key=lambda p: -col_hops(COL_SLOTS[p])):
         pt[p] = fold(tsum[:, p * OWN:(p + 1) * OWN])
         if p < LAST:
@@ -252,7 +260,7 @@
 
 def solution(mesh):
     n = (LAST + 1) * OWN
-    vmem, hbm = pl.BlockSpec(memory_space=pltpu.VMEM), pl.BlockSpec(memory_space=pl.ANY)
+    vmem, hbm = pl.BlockSpec(memory_space=pltpu.VMEM), pl.BlockSpec(memory_space=pltpu.HBM)
     slots = pltpu.VMEM((LAST + 1, 8, OWN), f32)
     call = pl.pallas_call(
         kernel,
@@ -284,7 +292,7 @@
     )
 
     def shards(target_state, target_mass, source_state, source_mass):
-        return call(target_state, target_mass.reshape(1, OWN), source_state, source_mass.reshape(1, OWN))
+        return call(*(pltpu.with_memory_space_constraint(x, pltpu.HBM) for x in (target_state, target_mass.reshape(1, OWN), source_state, source_mass.reshape(1, OWN))))
 
     spec = P(None, ("row", "col"))
     line = P(("row", "col"))

time: 41.6 us -> 39 us (0.938)
  local copies, waits for them, and re-layouts: 3.24 us -> 1.19 us
    unnamed x10 -> x2, local copies, waits for them, and re-layouts: 3.24 us -> 1.19 us
    pallas_call x1, Pallas kernels: 37.5 us -> 37.1 us  [shards(): call(*(pltpu.with_memory_space_constraint(x, pltpu.HBM) for x in (target_...]
where the time goes in v3:
time: 39 us; the launch traced here: 38.9 us
  Pallas kernels  37.1 us (95%)
  local copies, waits for them, and re-layouts  1.19 us (3%)
  between operations  0.64 us (2%)
    pallas_call x1, Pallas kernels, shards(): call(*(pltpu.with_memory_space_constraint(x, pltpu.HBM) for x in (target_...  37.1 us
    unnamed x2, local copies, waits for them, and re-layouts  1.19 us

profile of v3, /device:TPU:1, one launch (start us, length us, event | category | flops | bytes accessed | tf_op | source)
XLA Modules:
  0.0 38.9 jit_solution(16697661422615497560)
XLA Ops:
  0.6 37.1 %shard_map.59 = (f32[12,128]{1,0:T(8,128)S(1)}, f32[6,128]{1,0:T(8,128)S(1)}) custom-call(f32[12,128]{1,0:T(8,128)} %ts_hbm.1, f32[1,128]{1,0:T(1,128)} %bitcast.2, f32[12,128]{1,0:T(8,128)} %ss_hbm.1, f32[1,128]{1,0:T(1,128)} %bitcast.3), custom_call_target="tpu_custom_call" | custom-call | tf_op jit(solution)/shard_map/pallas_call | solution.py:295
  37.7 0.6 %copy.8 = f32[12,128]{1,0:T(8,128)} copy(f32[12,128]{1,0:T(8,128)S(1)} %get-tuple-element.4) | data formatting | bytes 12288
  38.3 0.6 %copy.9 = f32[6,128]{1,0:T(8,128)} copy(f32[6,128]{1,0:T(8,128)S(1)} %get-tuple-element.5) | data formatting | bytes 6144

commit v4 on v3

--- a/solution.py
+++ b/solution.py
@@ -56,60 +56,60 @@
     return accel, jerk
 
 
-def order(offsets, distance, groups):
-    left = sorted((o for o in offsets if any(o)), key=distance)
-    return groups(left) + [o for o in offsets if not any(o)]
-
-
-ROW_SIZES, COL_SIZES = (2, 8), (2, 4, 2)
-
-
-def offsets(sizes):
-    return list(np.ndindex(*sizes))
-
-
-def row_hops(o):
-    return 2 * o[0] + min(o[1], 8 - o[1])
-
-
-def col_hops(o):
-    return o[0] + min(o[1], 4 - o[1]) + 0.5 * o[2]
+TARGET_SIZES, SOURCE_SIZES = (4, 4), (8, 2)
+
+
+def target_hops(o):
+    return min(o[0], 4 - o[0]) + min(o[1], 4 - o[1])
+
+
+def source_hops(o):
+    return min(o[0], 8 - o[0]) + 0.5 * o[1]
 
 
 def spread(near):
-    return near[:4] + near[4:][::-1]
-
-
-ROW_SLOTS = order(offsets(ROW_SIZES), row_hops, spread)
-COL_SLOTS = order(offsets(COL_SIZES), col_hops, list)
+    return near[7:11] + near[11:][::-1] + near[3:7][::-1] + near[:3][::-1]
+
+
+def order(sizes, distance, arrange):
+    offsets = list(np.ndindex(*sizes))
+    return arrange(sorted(offsets[1:], key=distance)) + offsets[:1]
+
+
+TARGET_SLOTS = order(TARGET_SIZES, target_hops, lambda near: near[::-1])
+SOURCE_SLOTS = order(SOURCE_SIZES, source_hops, spread)
 
 
 def inverse(slots, sizes):
     return [slots.index(tuple(-a % n for a, n in zip(o, sizes))) for o in slots]
 
 
-ROW_BACK, COL_BACK = inverse(ROW_SLOTS, ROW_SIZES), inverse(COL_SLOTS, COL_SIZES)
+TARGET_BACK, SOURCE_BACK = inverse(TARGET_SLOTS, TARGET_SIZES), inverse(SOURCE_SLOTS, SOURCE_SIZES)
 LAST = 15
 BI = BK = 256
 WIDE = 2
 SLOTS = WIDE * BK // OWN
-
-
-def moved(index, offset, sizes):
-    out, unit = 0, 1
-    for o, n in reversed(list(zip(offset, sizes))):
-        out = out + lax.rem(lax.div(index, unit) + o, n) * unit
-        unit *= n
-    return out
+GROUP = 8
+
+
+def peers(row, col):
+    z, core, y = lax.rem(row, 8), lax.rem(col, 2), lax.rem(lax.div(col, 2), 4)
+    x = lax.div(row, 8) * 2 + lax.div(col, 8)
+    plane, line = [], []
+    for dx, dy in TARGET_SLOTS:
+        to_x, to_y = lax.rem(x + dx, 4), lax.rem(y + dy, 4)
+        plane.append((lax.div(to_x, 2) * 8 + z, (lax.rem(to_x, 2) * 4 + to_y) * 2 + core))
+    for dz, dc in SOURCE_SLOTS:
+        line.append((row - z + lax.rem(z + dz, 8), col - core + lax.rem(core + dc, 2)))
+    return plane, line
 
 
 def kernel(ts_hbm, tm_hbm, ss_hbm, sm_hbm, next_ref, pull_ref, ts_ref, tm_ref, ss_ref, sm_ref,
-           tgat, sgat, ft, fs, rc, rg, tc, tg, xb, xs, tsum, pt, ps, qt, qs, pair, turned, send, recv, load):
+           tgat, sgat, select, ft, fs, rc, rg, tc, tg, xb, xs, tsum, pt, ps, qt, qs, pair, turned, send, recv, load):
     row, col = lax.axis_index("row"), lax.axis_index("col")
-    row_peer = [(moved(row, o, ROW_SIZES), col) for o in ROW_SLOTS]
-    col_peer = [(row, moved(col, o, COL_SIZES)) for o in COL_SLOTS]
-    far = sorted([(-row_hops(ROW_SLOTS[p]), 0, p) for p in range(LAST)]
-                 + [(-col_hops(COL_SLOTS[p]), 1, p) for p in range(LAST)])
+    target_peer, source_peer = peers(row, col)
+    far = sorted([(-source_hops(SOURCE_SLOTS[p]), 0, p) for p in range(LAST)]
+                 + [(-target_hops(TARGET_SLOTS[p]), 1, p) for p in range(LAST)])
 
     loads = [pltpu.make_async_copy(a, b, load.at[n]) for n, (a, b) in enumerate(
         ((ts_hbm, ts_ref), (tm_hbm, tm_ref), (ss_hbm, ss_ref), (sm_hbm, sm_ref)))]
@@ -117,8 +117,13 @@
         copy.start()
     barrier = pltpu.get_barrier_semaphore()
     for _, axis, p in far:
-        pl.semaphore_signal(barrier, inc=1, device_id=(row_peer, col_peer)[axis][p], device_id_type=MESH)
+        pl.semaphore_signal(barrier, inc=1, device_id=(source_peer, target_peer)[axis][p], device_id_type=MESH)
     tsum[...] = jnp.zeros_like(tsum)
+    feature = lax.broadcasted_iota(jnp.int32, select.shape, 0)
+    axis = lax.broadcasted_iota(jnp.int32, select.shape, 1)
+    wanted = (axis >= OWN).astype(jnp.int32) + (axis >= 2 * OWN).astype(jnp.int32)
+    chosen = (feature == wanted) | (feature == wanted + 16) | (feature == wanted + 40)
+    select[...] = chosen.astype(f32).astype(bf16)
     for copy in loads:
         copy.wait()
     tgat[LAST] = predict(ts_ref[...], tm_ref[...] * (1.0 / 32768))
@@ -135,18 +140,21 @@
             src_ref=src, dst_ref=dst.at[p], send_sem=send.at[kind, 0],
             recv_sem=recv.at[kind, p], device_id=peer[0], device_id_type=MESH).wait_recv()
 
-    gathers = [(copy_to(sgat.at[LAST], sgat, 0, p, ROW_BACK, row_peer),
-                copy_to(tgat.at[LAST], tgat, 1, p, COL_BACK, col_peer))[axis] for _, axis, p in far]
+    gathers = [copy_to(tgat.at[LAST], tgat, 1, p, TARGET_BACK, target_peer) for p in range(LAST)]
+    gathers += [copy_to(sgat.at[LAST], sgat, 0, p, SOURCE_BACK, source_peer) for _, axis, p in far if axis == 0]
     for copy in gathers:
         copy.start()
-    source_returns = [copy_to(ps.at[p], qs, 2, p, ROW_BACK, row_peer) for p in range(LAST)]
-    target_returns = [copy_to(pt.at[p], qt, 3, p, COL_BACK, col_peer) for p in range(LAST)]
+    source_returns = [copy_to(ps.at[p], qs, 2, p, SOURCE_BACK, source_peer) for p in range(LAST)]
+    target_returns = [copy_to(pt.at[p], qt, 3, p, TARGET_BACK, target_peer) for p in range(LAST)]
 
     zeros = jnp.zeros((OWN - 48, OWN), f32)
+
+    def span(d):
+        return pl.ds(d * OWN if isinstance(d, int) else pl.multiple_of(d * OWN, OWN), OWN)
 
     def prepare_source(d):
         tile = sgat[d]
-        at = pl.ds(pl.multiple_of(d * OWN, OWN), OWN)
+        at = span(d)
         rc[:, at], rg[:, at] = moments(tile)
         x, v = tile[0:3], tile[3:6]
         vec = jnp.concatenate([-3.0 * v, -3.0 * x, 3.0 * jnp.sum(x * v, axis=0, keepdims=True), tile[6:7]], axis=0)
@@ -156,25 +164,26 @@
 
     def prepare_target(d):
         tile = tgat[d]
-        at = pl.ds(pl.multiple_of(d * OWN, OWN), OWN)
+        at = span(d)
         tc[:, at], tg[:, at] = moments(tile)
         x, v = tile[0:3], tile[3:6]
         vec = jnp.concatenate([x, v, tile[6:7], 3.0 * jnp.sum(x * v, axis=0, keepdims=True)], axis=0)
         h, m, l = pieces(vec)
-        ft[at, :] = jnp.concatenate([h, h, m, m, h, l, zeros], axis=0).T.astype(bf16)
-        for c in range(3):
-            xb[at, c * OWN:(c + 1) * OWN] = jnp.broadcast_to(tile[c:c + 1], (OWN, OWN)).T
+        features = jnp.concatenate([h, h, m, m, h, l, zeros], axis=0).T.astype(bf16)
+        ft[at, :] = features
+        xb[at, :] = dot(features, select[...], 1, 0)
 
     def arrive_targets(n, _):
-        for u in range(4):
-            @pl.when(n * 4 + u < LAST)
+        first = LAST + 1 - GROUP - n * GROUP
+        for u in range(GROUP):
+            @pl.when(first + u < LAST)
             def _():
-                arrived(tgat.at[LAST], tgat, 1, n * 4 + u, col_peer)
-        for u in range(4):
-            prepare_target(n * 4 + u)
+                arrived(tgat.at[LAST], tgat, 1, first + u, target_peer)
+        for u in range(GROUP):
+            prepare_target(first + u)
         return 0
 
-    lax.fori_loop(0, 4, arrive_targets, 0)
+    lax.fori_loop(0, (LAST + 1) // GROUP, arrive_targets, 0)
 
     def fold(total):
         return total[0:8] + total[8:16] + total[16:24]
@@ -185,18 +194,20 @@
         rck, rgk = rc[:, k], rg[:, k]
         return jnp.concatenate([rck, rck, rgk, rgk], axis=1)
 
+    passes = xs.shape[1] // (WIDE * BK)
+
     def strips(n, _):
         for u in range(SLOTS):
             p = n * SLOTS + u
 
             @pl.when(p < LAST)
             def _():
-                arrived(sgat.at[LAST], sgat, 0, p, row_peer)
+                arrived(sgat.at[LAST], sgat, 0, p, source_peer)
         for u in range(SLOTS):
             prepare_source(n * SLOTS + u)
         spans = [pl.ds(pl.multiple_of((n * WIDE + w) * BK, BK), BK) for w in range(WIDE)]
+        order = [(w, t) for w in range(WIDE) for t in range(tiles)]
         pulls = [jnp.zeros((32, BK), f32)] * WIDE
-        order = [(w, t) for w in range(WIDE) for t in range(tiles)]
         for m in range(len(order) + 1):
             if m < len(order):
                 w, t = order[m]
@@ -228,29 +239,31 @@
             folded = fold(pulls[w])
             for u in range(BK // OWN):
                 ps[n * SLOTS + w * (BK // OWN) + u] = folded[:, u * OWN:(u + 1) * OWN]
-        for m in range(LAST // SLOTS + 1):
+        for m in range(passes - 1):
             @pl.when(n == m)
             def _():
                 for copy in source_returns[SLOTS * m:SLOTS * m + SLOTS]:
                     copy.start()
         return 0
 
-    lax.fori_loop(0, xs.shape[1] // (WIDE * BK), strips, 0)
-    for p in sorted(range(LAST + 1), key=lambda p: -col_hops(COL_SLOTS[p])):
+    lax.fori_loop(0, passes, strips, 0)
+    for p in range(LAST + 1):
         pt[p] = fold(tsum[:, p * OWN:(p + 1) * OWN])
         if p < LAST:
             target_returns[p].start()
+    for copy in source_returns[SLOTS * (passes - 1):]:
+        copy.start()
     for copy in gathers + source_returns:
         copy.wait_send()
 
     for p in range(LAST):
-        arrived(ps.at[0], qs, 2, p, row_peer)
+        arrived(ps.at[0], qs, 2, p, source_peer)
     pull_ref[...] = jnp.concatenate(resolve(sum((qs[p] for p in range(LAST)), ps[LAST]), sgat[LAST]), axis=0)
 
     for copy in target_returns:
         copy.wait_send()
     for p in range(LAST):
-        arrived(pt.at[0], qt, 3, p, col_peer)
+        arrived(pt.at[0], qt, 3, p, target_peer)
     a1, j1 = resolve(sum((qt[p] for p in range(LAST)), pt[LAST]), tgat[LAST])
     x, v, a, j = ts_ref[0:3], ts_ref[3:6], ts_ref[6:9], ts_ref[9:12]
     v1 = v + 0.5 * STEP * (a + a1) + STEP * STEP / 12.0 * (j - j1)
@@ -274,6 +287,7 @@
             pltpu.VMEM((1, OWN), f32),
             slots,
             slots,
+            pltpu.VMEM((OWN, 3 * OWN), bf16),
             pltpu.VMEM((n, OWN), bf16),
             pltpu.VMEM((OWN, n), bf16),
             *[pltpu.VMEM((32, n), bf16)] * 4,

time: 39 us -> 37.3 us (0.956)
  Pallas kernels: 37.1 us -> 35.3 us
    pallas_call x1, Pallas kernels: 37.1 us -> 35.3 us  [shards(): call(*(pltpu.with_memory_space_constraint(x, pltpu.HBM) for x in (target_...]
where the time goes in v4:
time: 37.3 us; the launch traced here: 37.1 us
  Pallas kernels  35.3 us (95%)
  local copies, waits for them, and re-layouts  1.19 us (3%)
  between operations  0.64 us (2%)
    pallas_call x1, Pallas kernels, shards(): call(*(pltpu.with_memory_space_constraint(x, pltpu.HBM) for x in (target_...  35.3 us
    unnamed x2, local copies, waits for them, and re-layouts  1.19 us

profile of v4, /device:TPU:1, one launch (start us, length us, event | category | flops | bytes accessed | tf_op | source)
XLA Modules:
  0.0 37.1 jit_solution(16755021673192686128)
XLA Ops:
  0.6 35.3 %shard_map.59 = (f32[12,128]{1,0:T(8,128)S(1)}, f32[6,128]{1,0:T(8,128)S(1)}) custom-call(f32[12,128]{1,0:T(8,128)} %ts_hbm.1, f32[1,128]{1,0:T(1,128)} %bitcast.2, f32[12,128]{1,0:T(8,128)} %ss_hbm.1, f32[1,128]{1,0:T(1,128)} %bitcast.3), custom_call_target="tpu_custom_call" | custom-call | tf_op jit(solution)/shard_map/pallas_call | solution.py:309
  35.9 0.6 %copy.8 = f32[12,128]{1,0:T(8,128)} copy(f32[12,128]{1,0:T(8,128)S(1)} %get-tuple-element.4) | data formatting | bytes 12288
  36.6 0.6 %copy.9 = f32[6,128]{1,0:T(8,128)} copy(f32[6,128]{1,0:T(8,128)S(1)} %get-tuple-element.5) | data formatting | bytes 6144

commit v5 on v4

--- a/solution.py
+++ b/solution.py
@@ -68,7 +68,7 @@
 
 
 def spread(near):
-    return near[7:11] + near[11:][::-1] + near[3:7][::-1] + near[:3][::-1]
+    return near[::-1]
 
 
 def order(sizes, distance, arrange):
@@ -87,7 +87,7 @@
 TARGET_BACK, SOURCE_BACK = inverse(TARGET_SLOTS, TARGET_SIZES), inverse(SOURCE_SLOTS, SOURCE_SIZES)
 LAST = 15
 BI = BK = 256
-WIDE = 2
+WIDE = 4
 SLOTS = WIDE * BK // OWN
 GROUP = 8
 
@@ -207,7 +207,7 @@
             prepare_source(n * SLOTS + u)
         spans = [pl.ds(pl.multiple_of((n * WIDE + w) * BK, BK), BK) for w in range(WIDE)]
         order = [(w, t) for w in range(WIDE) for t in range(tiles)]
-        pulls = [jnp.zeros((32, BK), f32)] * WIDE
+        pulls = [jnp.zeros((8, BK), f32)] * WIDE
         for m in range(len(order) + 1):
             if m < len(order):
                 w, t = order[m]
@@ -232,11 +232,11 @@
                 tci, tgi = tc[:, i], tg[:, i]
                 here = [pair[(m - 1) % 2, x] for x in range(4)]
                 across = [turned[(m - 1) % 2, x] for x in range(4)]
-                pulls[w] = pulls[w] + dot(jnp.concatenate([tci, tci, tgi, tgi], axis=1),
-                                          jnp.concatenate(here, axis=0), 1, 0)
-                tsum[:, i] += dot(features(k), jnp.concatenate(across, axis=0), 1, 0)
+                pulls[w] = pulls[w] + fold(dot(jnp.concatenate([tci, tci, tgi, tgi], axis=1),
+                                          jnp.concatenate(here, axis=0), 1, 0))
+                tsum[:, i] += fold(dot(features(k), jnp.concatenate(across, axis=0), 1, 0))
         for w in range(WIDE):
-            folded = fold(pulls[w])
+            folded = pulls[w]
             for u in range(BK // OWN):
                 ps[n * SLOTS + w * (BK // OWN) + u] = folded[:, u * OWN:(u + 1) * OWN]
         for m in range(passes - 1):
@@ -248,7 +248,7 @@
 
     lax.fori_loop(0, passes, strips, 0)
     for p in range(LAST + 1):
-        pt[p] = fold(tsum[:, p * OWN:(p + 1) * OWN])
+        pt[p] = tsum[:, p * OWN:(p + 1) * OWN]
         if p < LAST:
             target_returns[p].start()
     for copy in source_returns[SLOTS * (passes - 1):]:
@@ -293,7 +293,7 @@
             *[pltpu.VMEM((32, n), bf16)] * 4,
             pltpu.VMEM((n, 3 * OWN), f32),
             pltpu.VMEM((8, n), f32),
-            pltpu.VMEM((32, n), f32),
+            pltpu.VMEM((8, n), f32),
             *[slots] * 4,
             pltpu.VMEM((2, 4, BI, BK), bf16),
             pltpu.VMEM((2, 4, BK, BI), bf16),

time: 37.3 us -> 36.3 us (0.973)
  Pallas kernels: 35.3 us -> 34.4 us
    pallas_call x1, Pallas kernels: 35.3 us -> 34.4 us  [shards(): call(*(pltpu.with_memory_space_constraint(x, pltpu.HBM) for x in (target_...]
where the time goes in v5:
time: 36.3 us; the launch traced here: 36.2 us
  Pallas kernels  34.4 us (95%)
  local copies, waits for them, and re-layouts  1.19 us (3%)
  between operations  0.64 us (2%)
    pallas_call x1, Pallas kernels, shards(): call(*(pltpu.with_memory_space_constraint(x, pltpu.HBM) for x in (target_...  34.4 us
    unnamed x2, local copies, waits for them, and re-layouts  1.19 us

profile of v5, /device:TPU:1, one launch (start us, length us, event | category | flops | bytes accessed | tf_op | source)
XLA Modules:
  0.0 36.2 jit_solution(18178279808677916821)
XLA Ops:
  0.6 34.4 %shard_map.59 = (f32[12,128]{1,0:T(8,128)S(1)}, f32[6,128]{1,0:T(8,128)S(1)}) custom-call(f32[12,128]{1,0:T(8,128)} %ts_hbm.1, f32[1,128]{1,0:T(1,128)} %bitcast.2, f32[12,128]{1,0:T(8,128)} %ss_hbm.1, f32[1,128]{1,0:T(1,128)} %bitcast.3), custom_call_target="tpu_custom_call" | custom-call | tf_op jit(solution)/shard_map/pallas_call | solution.py:309
  35.0 0.6 %copy.8 = f32[12,128]{1,0:T(8,128)} copy(f32[12,128]{1,0:T(8,128)S(1)} %get-tuple-element.4) | data formatting | bytes 12288
  35.6 0.6 %copy.9 = f32[6,128]{1,0:T(8,128)} copy(f32[6,128]{1,0:T(8,128)S(1)} %get-tuple-element.5) | data formatting | bytes 6144

commit v6 on v5

--- a/solution.py
+++ b/solution.py
@@ -147,7 +147,7 @@
     source_returns = [copy_to(ps.at[p], qs, 2, p, SOURCE_BACK, source_peer) for p in range(LAST)]
     target_returns = [copy_to(pt.at[p], qt, 3, p, TARGET_BACK, target_peer) for p in range(LAST)]
 
-    zeros = jnp.zeros((OWN - 48, OWN), f32)
+    zeros, pad = jnp.zeros((16, OWN), f32), jnp.zeros((64, OWN), f32)
 
     def span(d):
         return pl.ds(d * OWN if isinstance(d, int) else pl.multiple_of(d * OWN, OWN), OWN)
@@ -169,7 +169,7 @@
         x, v = tile[0:3], tile[3:6]
         vec = jnp.concatenate([x, v, tile[6:7], 3.0 * jnp.sum(x * v, axis=0, keepdims=True)], axis=0)
         h, m, l = pieces(vec)
-        features = jnp.concatenate([h, h, m, m, h, l, zeros], axis=0).T.astype(bf16)
+        features = jnp.concatenate([h, h, m, m, h, l, zeros, pad], axis=0).T.astype(bf16)
         ft[at, :] = features
         xb[at, :] = dot(features, select[...], 1, 0)
 
@@ -185,14 +185,13 @@
 
     lax.fori_loop(0, (LAST + 1) // GROUP, arrive_targets, 0)
 
+    def fold_two(total):
+        return total[0:8] + total[8:16]
+
     def fold(total):
         return total[0:8] + total[8:16] + total[16:24]
 
     tiles = tsum.shape[1] // BI
-
-    def features(k):
-        rck, rgk = rc[:, k], rg[:, k]
-        return jnp.concatenate([rck, rck, rgk, rgk], axis=1)
 
     passes = xs.shape[1] // (WIDE * BK)
 
@@ -212,7 +211,7 @@
             if m < len(order):
                 w, t = order[m]
                 k, i = spans[w], slice(t * BI, (t + 1) * BI)
-                dw = dot(ft[i, :], fs[:, k], 1, 0)
+                dw = dot(ft[i, 0:64], fs[:, k], 1, 0)
                 s = SOFTEN
                 for c in range(3):
                     left = xb[i, c * OWN:(c + 1) * OWN]
@@ -232,9 +231,14 @@
                 tci, tgi = tc[:, i], tg[:, i]
                 here = [pair[(m - 1) % 2, x] for x in range(4)]
                 across = [turned[(m - 1) % 2, x] for x in range(4)]
-                pulls[w] = pulls[w] + fold(dot(jnp.concatenate([tci, tci, tgi, tgi], axis=1),
-                                          jnp.concatenate(here, axis=0), 1, 0))
-                tsum[:, i] += fold(dot(features(k), jnp.concatenate(across, axis=0), 1, 0))
+                rck, rgk = rc[:, k], rg[:, k]
+                pulls[w] = (pulls[w] + fold(dot(jnp.concatenate([tci, tgi], axis=1),
+                                                jnp.concatenate(here[::2], axis=0), 1, 0))
+                            + fold_two(dot(jnp.concatenate([tci[0:16], tgi[0:16]], axis=1),
+                                           jnp.concatenate(here[1::2], axis=0), 1, 0)))
+                tsum[:, i] += (fold(dot(jnp.concatenate([rck, rgk], axis=1), jnp.concatenate(across[::2], axis=0), 1, 0))
+                               + fold_two(dot(jnp.concatenate([rck[0:16], rgk[0:16]], axis=1),
+                                              jnp.concatenate(across[1::2], axis=0), 1, 0)))
         for w in range(WIDE):
             folded = pulls[w]
             for u in range(BK // OWN):
@@ -289,7 +293,7 @@
             slots,
             pltpu.VMEM((OWN, 3 * OWN), bf16),
             pltpu.VMEM((n, OWN), bf16),
-            pltpu.VMEM((OWN, n), bf16),
+            pltpu.VMEM((64, n), bf16),
             *[pltpu.VMEM((32, n), bf16)] * 4,
             pltpu.VMEM((n, 3 * OWN), f32),
             pltpu.VMEM((8, n), f32),

time: 36.3 us -> 35.8 us (0.986)
  Pallas kernels: 34.4 us -> 33.9 us
    pallas_call x1, Pallas kernels: 34.4 us -> 33.9 us  [shards(): call(*(pltpu.with_memory_space_constraint(x, pltpu.HBM) for x in (target_...]
where the time goes in v6:
time: 35.8 us; the launch traced here: 35.7 us
  Pallas kernels  33.9 us (95%)
  local copies, waits for them, and re-layouts  1.19 us (3%)
  between operations  0.64 us (2%)
    pallas_call x1, Pallas kernels, shards(): call(*(pltpu.with_memory_space_constraint(x, pltpu.HBM) for x in (target_...  33.9 us
    unnamed x2, local copies, waits for them, and re-layouts  1.19 us

profile of v6, /device:TPU:1, one launch (start us, length us, event | category | flops | bytes accessed | tf_op | source)
XLA Modules:
  0.0 35.7 jit_solution(14927269703254213072)
XLA Ops:
  0.6 33.9 %shard_map.59 = (f32[12,128]{1,0:T(8,128)S(1)}, f32[6,128]{1,0:T(8,128)S(1)}) custom-call(f32[12,128]{1,0:T(8,128)} %ts_hbm.1, f32[1,128]{1,0:T(1,128)} %bitcast.2, f32[12,128]{1,0:T(8,128)} %ss_hbm.1, f32[1,128]{1,0:T(1,128)} %bitcast.3), custom_call_target="tpu_custom_call" | custom-call | tf_op jit(solution)/shard_map/pallas_call | solution.py:313
  34.5 0.6 %copy.8 = f32[12,128]{1,0:T(8,128)} copy(f32[12,128]{1,0:T(8,128)S(1)} %get-tuple-element.4) | data formatting | bytes 12288
  35.1 0.6 %copy.9 = f32[6,128]{1,0:T(8,128)} copy(f32[6,128]{1,0:T(8,128)S(1)} %get-tuple-element.5) | data formatting | bytes 6144

commit v7 on v6

--- a/solution.py
+++ b/solution.py
@@ -147,7 +147,7 @@
     source_returns = [copy_to(ps.at[p], qs, 2, p, SOURCE_BACK, source_peer) for p in range(LAST)]
     target_returns = [copy_to(pt.at[p], qt, 3, p, TARGET_BACK, target_peer) for p in range(LAST)]
 
-    zeros, pad = jnp.zeros((16, OWN), f32), jnp.zeros((64, OWN), f32)
+    zeros = jnp.zeros((OWN - 48, OWN), f32)
 
     def span(d):
         return pl.ds(d * OWN if isinstance(d, int) else pl.multiple_of(d * OWN, OWN), OWN)
@@ -159,7 +159,7 @@
         x, v = tile[0:3], tile[3:6]
         vec = jnp.concatenate([-3.0 * v, -3.0 * x, 3.0 * jnp.sum(x * v, axis=0, keepdims=True), tile[6:7]], axis=0)
         h, m, l = pieces(vec)
-        fs[:, at] = jnp.concatenate([h, m, h, m, l, h, zeros], axis=0).astype(bf16)
+        fs[:, at] = jnp.concatenate([h, m, h, m, l, h], axis=0).astype(bf16)
         xs[:, at] = tile
 
     def prepare_target(d):
@@ -169,7 +169,7 @@
         x, v = tile[0:3], tile[3:6]
         vec = jnp.concatenate([x, v, tile[6:7], 3.0 * jnp.sum(x * v, axis=0, keepdims=True)], axis=0)
         h, m, l = pieces(vec)
-        features = jnp.concatenate([h, h, m, m, h, l, zeros, pad], axis=0).T.astype(bf16)
+        features = jnp.concatenate([h, h, m, m, h, l, zeros], axis=0).T.astype(bf16)
         ft[at, :] = features
         xb[at, :] = dot(features, select[...], 1, 0)
 
@@ -211,7 +211,7 @@
             if m < len(order):
                 w, t = order[m]
                 k, i = spans[w], slice(t * BI, (t + 1) * BI)
-                dw = dot(ft[i, 0:64], fs[:, k], 1, 0)
+                dw = dot(ft[i, 0:48], fs[:, k], 1, 0)
                 s = SOFTEN
                 for c in range(3):
                     left = xb[i, c * OWN:(c + 1) * OWN]
@@ -293,7 +293,7 @@
             slots,
             pltpu.VMEM((OWN, 3 * OWN), bf16),
             pltpu.VMEM((n, OWN), bf16),
-            pltpu.VMEM((64, n), bf16),
+            pltpu.VMEM((48, n), bf16),
             *[pltpu.VMEM((32, n), bf16)] * 4,
             pltpu.VMEM((n, 3 * OWN), f32),
             pltpu.VMEM((8, n), f32),

time: 35.8 us -> 36 us (level)
  no operation moved by 1% of the time
where the time goes in v7:
time: 36 us; the launch traced here: 35.9 us
  Pallas kernels  34.1 us (95%)
  local copies, waits for them, and re-layouts  1.19 us (3%)
  between operations  0.64 us (2%)
    pallas_call x1, Pallas kernels, shards(): call(*(pltpu.with_memory_space_constraint(x, pltpu.HBM) for x in (target_...  34.1 us
    unnamed x2, local copies, waits for them, and re-layouts  1.19 us

profile of v7, /device:TPU:1, one launch (start us, length us, event | category | flops | bytes accessed | tf_op | source)
XLA Modules:
  0.0 35.9 jit_solution(12072373229672998918)
XLA Ops:
  0.6 34.1 %shard_map.59 = (f32[12,128]{1,0:T(8,128)S(1)}, f32[6,128]{1,0:T(8,128)S(1)}) custom-call(f32[12,128]{1,0:T(8,128)} %ts_hbm.1, f32[1,128]{1,0:T(1,128)} %bitcast.2, f32[12,128]{1,0:T(8,128)} %ss_hbm.1, f32[1,128]{1,0:T(1,128)} %bitcast.3), custom_call_target="tpu_custom_call" | custom-call | tf_op jit(solution)/shard_map/pallas_call | solution.py:313
  34.7 0.6 %copy.8 = f32[12,128]{1,0:T(8,128)} copy(f32[12,128]{1,0:T(8,128)S(1)} %get-tuple-element.4) | data formatting | bytes 12288
  35.3 0.6 %copy.9 = f32[6,128]{1,0:T(8,128)} copy(f32[6,128]{1,0:T(8,128)S(1)} %get-tuple-element.5) | data formatting | bytes 6144
